TPU v7x, 32 devices: a whole 2x2x4 slice. The times are simulated.
32 devices in a mesh: req: 4 (over y, core), tp: 8 (over z, x).
Axes of the slice: x: 2, y: 2, z: 4, core: 2. Of those that a mesh axis runs over, the one named last changes fastest.
Arguments:
- queries: bfloat16 [16, 32, 4096], P('req'), may hold values from -128 to 128
- cache_keys: bfloat16 [16, 4096, 512], P('req', 'tp'), may hold values from -4 to 4
- cache_values: bfloat16 [16, 4096, 512], P('req', 'tp'), may hold values from -5 to 5
- tree_keys: bfloat16 [16, 32, 512], P('req', 'tp'), may hold values from -5 to 5
- tree_values: bfloat16 [16, 32, 512], P('req', 'tp'), may hold values from -5 to 5
- parents: int32 [16, 32], P('req'), may hold values from -1 to 30, as said below
- lengths: int32 [16], P('req'), may hold values from 2 to 4096
- accepted_leaf: int32 [16], P('req'), may hold values from 0 to 31
- residual: bfloat16 [16, 32, 8192], P('req', None, 'tp'), may hold values from -12 to 12
- norm_gain: float32 [8192], replicated, may hold values from 0.5 to 4
- out_weight: bfloat16 [4096, 8192], P('tp'), may hold values from -0.09375 to 0.09375
- prev_feature: bfloat16 [16, 8192], P('req'), may hold values from -5 to 5
- draft_weight: bfloat16 [8192, 8192], P('req', 'tp'), may hold values from -0.0625 to 0.0625
- first_moment: float32 [8192, 8192], P('req', 'tp'), may hold values from -5 to 5
- second_moment: float32 [8192, 8192], P('req', 'tp'), may hold values from 0.25 to 4
Outputs:
- features: bfloat16 [16, 32, 8192], P('req', None, 'tp')
- new_weight: bfloat16 [8192, 8192], P('req', 'tp')
- new_first: float32 [8192, 8192], P('req', 'tp')
- new_second: float32 [8192, 8192], P('req', 'tp')
- draft_loss: float32 [], replicated
Inputs may be any that keep to these rules, and one draw needn't show every extreme that they name: parents[r, 0] = -1; for i of 1 or more, parents[r, i] lies in 0 to i - 1; node 31 is a child of node 30.
All inputs are finite; a program needn't handle non-finite values.
Results may differ from a plain program's by a relative error of at most 0.014.
Values may be sent and summed in bfloat16 or wider, within the bound.
A program may use at most 192 MiB of HBM per device.

v0:
```python
import math

import jax
import jax.numpy as jnp
from jax import lax
from jax.sharding import PartitionSpec as P

HEADS = 32
KV_HEADS = 4
HEAD = 128
NODES = 32
CACHE = 4096


NEG_FILL = -1e30
NORM_EPSILON = 1e-06
BETA_ONE = 0.9
BETA_TWO = 0.95
CORRECT_ONE = 1.0 - 0.9**10
CORRECT_TWO = 1.0 - 0.95**10
LEARN_RATE = 0.001


def closure(parents):
    node_count = parents.shape[-1]
    onehot = (parents[:, :, None] == jnp.arange(node_count, dtype=jnp.int32)[None, None, :]).astype(
        jnp.float32
    )
    reach_map = jnp.eye(node_count, dtype=jnp.float32)[None] + onehot
    for repeat in range(node_count.bit_length()):
        reach_map = jnp.minimum(
            jnp.einsum("rij,rjk->rik", reach_map, reach_map, precision=lax.Precision.HIGHEST), 1.0
        )
    return reach_map


def body(
    queries,
    cache_keys,
    cache_values,
    tree_keys,
    tree_values,
    parents,
    lengths,
    accepted_leaf,
    residual,
    norm_gain,
    out_weight,
    prev_feature,
    draft_weight,
    first_moment,
    second_moment,
):
    full_residual = lax.all_gather(residual, "tp", axis=2, tiled=True)
    requests = queries.shape[0]
    row_count = requests * NODES
    groups = HEADS // KV_HEADS
    score_scale = 1.0 / math.sqrt(HEAD)
    tp_rank = lax.axis_index("tp")
    cache_span = cache_keys.shape[1]
    tree_span = tree_keys.shape[1]
    reach_map = closure(parents)
    query_view = queries.reshape(requests, NODES, KV_HEADS, groups, HEAD)
    cache_view = cache_keys.reshape(requests, cache_span, KV_HEADS, HEAD)
    tree_view = tree_keys.reshape(requests, tree_span, KV_HEADS, HEAD)
    cache_scores = (
        jnp.einsum("rnkgd,rckd->rkgnc", query_view, cache_view, preferred_element_type=jnp.float32)
        * score_scale
    )
    tree_scores = (
        jnp.einsum("rnkgd,rjkd->rkgnj", query_view, tree_view, preferred_element_type=jnp.float32)
        * score_scale
    )
    positions = tp_rank * cache_span + jnp.arange(cache_span, dtype=jnp.int32)
    cache_live = (positions[None, :] < lengths[:, None])[:, None, None, None, :]
    visible = lax.dynamic_slice_in_dim(reach_map, tp_rank * tree_span, tree_span, 2)
    tree_live = (visible > 0.5)[:, None, None, :, :]
    cache_scores = jnp.where(cache_live, cache_scores, NEG_FILL)
    tree_scores = jnp.where(tree_live, tree_scores, NEG_FILL)
    local_top = jnp.maximum(jnp.max(cache_scores, axis=-1), jnp.max(tree_scores, axis=-1))
    row_top = lax.pmax(local_top, "tp")
    cache_probs = jnp.where(cache_live, jnp.exp(cache_scores - row_top[..., None]), 0.0).astype(
        jnp.bfloat16
    )
    tree_probs = jnp.where(tree_live, jnp.exp(tree_scores - row_top[..., None]), 0.0).astype(
        jnp.bfloat16
    )
    totals = jnp.sum(cache_probs, axis=-1, dtype=jnp.float32) + jnp.sum(
        tree_probs, axis=-1, dtype=jnp.float32
    )
    value_view = cache_values.reshape(requests, cache_span, KV_HEADS, HEAD)
    tree_value_view = tree_values.reshape(requests, tree_span, KV_HEADS, HEAD)
    weighted = jnp.einsum(
        "rkgnc,rckd->rnkgd", cache_probs, value_view, preferred_element_type=jnp.float32
    )
    weighted = weighted + jnp.einsum(
        "rkgnj,rjkd->rnkgd", tree_probs, tree_value_view, preferred_element_type=jnp.float32
    )
    weighted = weighted.reshape(row_count, HEADS * HEAD)
    totals = jnp.transpose(totals, (0, 3, 1, 2)).reshape(row_count, HEADS)
    head_sums, head_totals = (
        lax.psum_scatter(weighted, "tp", scatter_dimension=1, tiled=True),
        lax.psum_scatter(totals, "tp", scatter_dimension=1, tiled=True),
    )
    own_heads = head_totals.shape[1]
    attended = (head_sums.reshape(row_count, own_heads, HEAD) / head_totals[:, :, None]).astype(
        jnp.bfloat16
    )
    partial_value = jnp.dot(
        attended.reshape(row_count, own_heads * HEAD),
        out_weight,
        preferred_element_type=jnp.float32,
    )
    partial_value = lax.optimization_barrier(partial_value.astype(jnp.bfloat16)).astype(jnp.float32)
    model_width = partial_value.shape[1]
    block_width = model_width // lax.axis_size("tp")
    summed = lax.psum(partial_value.astype(jnp.bfloat16), "tp").astype(jnp.float32)
    mixed = full_residual.reshape(row_count, model_width).astype(jnp.float32) + summed
    mean_sq = jnp.mean(mixed * mixed, axis=1, keepdims=True)
    features = (mixed * lax.rsqrt(mean_sq + NORM_EPSILON) * norm_gain[None, :]).astype(jnp.bfloat16)
    own_block = lax.dynamic_slice_in_dim(features, tp_rank * block_width, block_width, 1)
    feature_table = jnp.concatenate(
        [prev_feature[:, None, :], features.reshape(requests, NODES, model_width)], axis=1
    )
    inputs = jnp.take_along_axis(feature_table, (parents + 1)[:, :, None], axis=1).reshape(
        row_count, model_width
    )
    leaf_hot = (accepted_leaf[:, None] == jnp.arange(NODES, dtype=jnp.int32)[None, :]).astype(
        jnp.float32
    )
    accepted = jnp.einsum("rn,rnj->rj", leaf_hot, reach_map, precision=lax.Precision.HIGHEST)
    fill_share = 0.5 + lengths.astype(jnp.float32) / CACHE
    weights = ((1.0 + 3.0 * accepted) * fill_share[:, None]).reshape(row_count, 1)
    columns = inputs
    predicted = jnp.dot(
        columns,
        lax.all_gather(draft_weight, "req", axis=0, tiled=True),
        preferred_element_type=jnp.float32,
    )
    pred_error = predicted - own_block.astype(jnp.float32)
    scaled_err = (weights * pred_error).astype(jnp.bfloat16)
    columns = inputs
    gradient = lax.psum_scatter(
        lax.dot_general(
            columns, scaled_err, (((0,), (0,)), ((), ())), preferred_element_type=jnp.float32
        ),
        "req",
        scatter_dimension=0,
        tiled=True,
    )
    square_total, error_total = lax.psum(
        (jnp.sum(gradient * gradient), jnp.sum(weights * pred_error * pred_error)), ("req", "tp")
    )
    draft_loss = 0.5 * error_total / (row_count * lax.axis_size("req") * model_width)
    grad_norm = jnp.sqrt(square_total) + 1e-06
    clip_factor = jnp.minimum(1.0, model_width / grad_norm)
    clipped = gradient * clip_factor
    new_first = BETA_ONE * first_moment + (1.0 - BETA_ONE) * clipped
    new_second = BETA_TWO * second_moment + (1.0 - BETA_TWO) * clipped * clipped
    direction = new_first / CORRECT_ONE / (jnp.sqrt(new_second / CORRECT_TWO) + 1e-08)
    new_weight = (draft_weight.astype(jnp.float32) - LEARN_RATE * direction).astype(jnp.bfloat16)
    return (
        own_block.reshape(requests, NODES, block_width),
        new_weight,
        new_first,
        new_second,
        draft_loss,
    )


def solution(mesh):
    placed = (
        P("req", None, None),
        P("req", "tp", None),
        P("req", "tp", None),
        P("req", "tp", None),
        P("req", "tp", None),
        P("req", None),
        P("req"),
        P("req"),
        P("req", None, "tp"),
        P(),
        P("tp", None),
        P("req", None),
        P("req", "tp"),
        P("req", "tp"),
        P("req", "tp"),
    )
    return jax.shard_map(
        body,
        mesh=mesh,
        in_specs=placed,
        out_specs=(P("req", None, "tp"), P("req", "tp"), P("req", "tp"), P("req", "tp"), P()),
        check_vma=False,
    )
```

profile of v0, /device:TPU:0, one launch (start us, length us, event | category | flops | bytes accessed | tf_op | source)
XLA Modules:
  0.0 730.3 jit_solution(4477468874210624843)
XLA Ops:
  9.4 1.4 copy.99
  10.9 2.0 reshape.107
  12.9 2.5 reshape.110
  15.6 1.5 fusion.34
  17.1 6.7 bitcast_reduce_fusion
  23.8 39.3 %pmax.7 = f32[4,4,8,32]{3,2,1,0:T(8,128)S(1)} all-reduce(f32[4,4,8,32]{3,2,1,0:T(8,128)S(1)} %max.5), channel_id=1, replica_groups=mesh['req'=4,'tp'=8] {'tp'}, use_global_device_ids=true, to_apply=%region_2.3 | all-reduce | flops 4096 | bytes 32768 | tf_op jit(solution)/shard_map/pmax | solution.py:81
  63.6 4.7 add_bitcast_fusion
  69.5 1.5 reshape.112
  72.1 4.7 convert_reduce_fusion
  78.2 33.4 %all-reduce = f32[128,32]{0,1:T(8,128)S(1)} all-reduce(f32[128,32]{0,1:T(8,128)S(1)} %reshape.113), channel_id=3, replica_groups=mesh['req'=4,'tp'=8] {'tp'}, use_global_device_ids=true, to_apply=%region_6.7.clone | all-reduce | flops 4096 | bytes 32768
  111.8 24.9 %reduce-scatter.3.cloned.1.call-done = f32[128,512]{1,0:T(8,128)} async-done(((f32[128,4096]{1,0:T(8,128)}), f32[128,512]{1,0:T(8,128)}) %reduce-scatter.3.cloned.1.call-update) | async-done | bytes 262160 | tf_op jit(solution)/shard_map/reduce_scatter | solution.py:102
  136.9 6.1 convolution_convert_fusion
  144.4 42.8 %all-gather.3.cloned.1.call-done = bf16[4,32,8192]{2,1,0:T(8,128)(2,1)} async-done(((bf16[4,32,1024]{2,1,0:T(8,128)(2,1)}), bf16[4,32,8192]{2,1,0:T(8,128)(2,1)}) %all-gather.3.cloned.1.call-update) | async-done | bytes 2097168 | tf_op jit(solution)/shard_map/all_gather | solution.py:54
  187.2 104.6 %all-reduce.4.cloned.1.call-done = bf16[128,8192]{1,0:T(8,128)(2,1)} async-done(((bf16[128,8192]{1,0:T(8,128)(2,1)}), bf16[128,8192]{1,0:T(8,128)(2,1)}) %all-reduce.4.cloned.1.call-update) | async-done | bytes 2097168 | tf_op jit(solution)/shard_map/psum | solution.py:117
  291.8 3.1 multiply_reduce_fusion.1
  295.9 1.6 copy.74
  298.9 8.2 %gather_fusion = bf16[128,8192]{1,0:T(8,128)(2,1)} fusion(bf16[4,33,8192]{2,0,1:T(4,128)(2,1)S(1)} %pad_maximum_fusion, s32[128]{0:T(128)S(1)} %reshape.117), kind=kCustom, calls=%fused_computation | custom fusion | bytes 4195328 | tf_op jit(solution)/shard_map/jit(take_along_axis)/gather | solution.py:125
  308.2 90.7 %all-gather.5.cloned.1.call-done = bf16[8192,1024]{1,0:T(8,128)(2,1)} async-done(((bf16[2048,1024]{1,0:T(8,128)(2,1)}), bf16[8192,1024]{1,0:T(8,128)(2,1)}) %all-gather.5.cloned.1.call-update) | async-done | bytes 16777232 | tf_op jit(solution)/shard_map/all_gather | solution.py:137
  398.9 9.7 %fusion.15 = (f32[]{:T(128)}, f32[128,1024]{1,0:T(8,128)S(1)}) fusion(f32[128]{0:T(128)S(1)} %mul.137, bf16[128,1024]{1,0:T(8,128)(2,1)S(1)} %constant_dynamic-slice_fusion.1, bf16[8192,1024]{1,0:T(8,128)(2,1)} %all-gather.5.cloned.1.call-done, bf16[128,8192]{1,0:T(8,128)(2,1)} %gather_fusion, pred[128]{0:T(512)(128)(4,1)S(1)} %broadcast_in_dim.74), kind=kOutput, calls=%fused_computation.39 | convolution fusion | flops 2149187584 | bytes 19661444 | tf_op jit(solution)/shard_map/dot_general | solution.py:135
  408.6 13.2 %fusion.14 = f32[8192,1024]{1,0:T(8,128)} fusion(bf16[128,8192]{1,0:T(8,128)(2,1)S(1)} %copy-done.3, pred[128]{0:T(512)(128)(4,1)S(1)} %broadcast_in_dim.74, f32[128,1024]{1,0:T(8,128)S(1)} %get-tuple-element.15, f32[128]{0:T(128)S(1)} %mul.137), kind=kOutput, calls=%fused_computation.36 | convolution fusion | flops 2148794368 | bytes 36176512 | tf_op jit(solution)/shard_map/dot_general | solution.py:144
  421.8 235.0 %reduce-scatter.5.cloned.1.call-done = f32[2048,1024]{1,0:T(8,128)} async-done(((f32[8192,1024]{1,0:T(8,128)}), f32[2048,1024]{1,0:T(8,128)}) %reduce-scatter.5.cloned.1.call-update) | async-done | bytes 8388624 | tf_op jit(solution)/shard_map/reduce_scatter | solution.py:143
  656.8 6.1 multiply_reduce_fusion
  663.0 39.6 %all-reduce.1 = (f32[]{:T(128)}, f32[]{:T(128)}) all-reduce(f32[]{:T(128)} %multiply_reduce_fusion, f32[]{:T(128)} %get-tuple-element.14), channel_id=1, replica_groups=mesh['req'=4,'tp'=8] {'req','tp'}, use_global_device_ids=true, to_apply=%region_11.12 | all-reduce | flops 2 | bytes 16 | tf_op jit(solution)/shard_map/psum | solution.py:151
  703.9 18.7 %subtract_convert_fusion = (bf16[2048,1024]{1,0:T(8,128)(2,1)}, f32[2048,1024]{1,0:T(8,128)}, f32[2048,1024]{1,0:T(8,128)}) fusion(bf16[2048,1024]{1,0:T(8,128)(2,1)} %param.27, f32[2048,1024]{1,0:T(8,128)} %reduce-scatter.5.cloned.1.call-done, f32[]{:T(128)S(6)} %min.27, f32[2048,1024]{1,0:T(8,128)} %param.28, f32[2048,1024]{1,0:T(8,128)} %param.29), kind=kLoop, calls=%fused_computation.9 | loop fusion | flops 33554432 | bytes 50331652 | tf_op jit(solution)/shard_map/convert_element_type | solution.py:161
  (74 shorter events, 10.9 us)
Async XLA Ops:
  7.2 55.9 %copy-start = (bf16[4,4,512]{2,1,0:T(4,128)(2,1)S(1)}, bf16[4,4,512]{2,1,0:T(4,128)(2,1)}, u32[]{:S(2)}) copy-start(bf16[4,4,512]{2,1,0:T(4,128)(2,1)} %param.19) | copy-start | bytes 49156
  7.2 3.7 copy-start.6
  7.2 129.5 %reduce-scatter.3.cloned.1.call-start = ((), (), s32[]{:S(2)}) async-start(), calls=%async_computation.3 | async-start | bytes 2359296 | tf_op jit(solution)/shard_map/reduce_scatter | solution.py:102
  10.9 4.6 copy-start.11
  10.9 4.7 copy-start.12
  71.0 116.2 %all-gather.3.cloned.1.call-start = ((), (), s32[]{:S(2)}) async-start(), calls=%async_computation.2 | async-start | bytes 2359296 | tf_op jit(solution)/shard_map/all_gather | solution.py:54
  71.8 220.0 %all-reduce.4.cloned.1.call-start = ((), (), s32[]{:S(2)}) async-start(), calls=%async_computation.4 | async-start | bytes 4194304 | tf_op jit(solution)/shard_map/psum | solution.py:117
  72.1 4.9 copy-start.14
  142.9 0.8 copy-start.10
  142.9 1.1 copy-start.13
  143.0 152.0 %copy-start.9 = (f32[8192]{0:T(1024)S(1)}, f32[8192]{0:T(1024)}, u32[]{:S(2)}) copy-start(f32[8192]{0:T(1024)} %param.24) | copy-start | bytes 98308
  143.0 255.9 %all-gather.5.cloned.1.call-start = ((), (), s32[]{:S(2)}) async-start(), calls=%async_computation.5 | async-start | bytes 20971520 | tf_op jit(solution)/shard_map/all_gather | solution.py:137
  143.6 513.2 %reduce-scatter.5.cloned.1.call-start = ((), (), s32[]{:S(2)}) async-start(), calls=%async_computation.6 | async-start | bytes 41943040 | tf_op jit(solution)/shard_map/reduce_scatter | solution.py:143
  187.2 107.7 %copy-start.4 = (bf16[4,32,8192]{2,1,0:T(8,128)(2,1)S(1)}, bf16[4,32,8192]{2,1,0:T(8,128)(2,1)}, u32[]{:S(2)}) copy-start(bf16[4,32,8192]{2,1,0:T(8,128)(2,1)} %all-gather.3.cloned.1.call-done) | copy-start | bytes 6291460
  291.8 3.2 copy-start.5
  295.0 2.6 copy-start.8
  295.9 1.6 copy-start.2
  308.2 100.4 %copy-start.7 = (bf16[128,1024]{1,0:T(8,128)(2,1)}, bf16[128,1024]{1,0:T(8,128)(2,1)S(1)}, u32[]{:S(2)}) copy-start(bf16[128,1024]{1,0:T(8,128)(2,1)S(1)} %constant_dynamic-slice_fusion.1) | copy-start | bytes 786436
  308.2 100.4 %copy-start.3 = (bf16[128,8192]{1,0:T(8,128)(2,1)S(1)}, bf16[128,8192]{1,0:T(8,128)(2,1)}, u32[]{:S(2)}) copy-start(bf16[128,8192]{1,0:T(8,128)(2,1)} %gather_fusion) | copy-start | bytes 6291460
  703.9 18.7 %copy-start.1 = (bf16[4,4,512]{2,1,0:T(4,128)(2,1)S(1)}, bf16[4,4,512]{2,1,0:T(4,128)(2,1)}, u32[]{:S(2)}) copy-start(bf16[4,4,512]{2,1,0:T(4,128)(2,1)} %param.19) | copy-start | bytes 49156
Sparse Core Ops, SparseCore 0:
  71.2 65.4 reduce-scatter.2
  138.9 48.3 all-gather.2
  191.4 100.3 all-reduce.3
  293.2 105.6 all-gather.4
  421.9 234.8 reduce-scatter.4
where the time goes:
time: 731 us; the launch traced here: 730 us
  waiting for transfers between devices  499 us (68%)
  blocking collectives  112 us (15%)
  matrix products  44.6 us (6%)
  other arithmetic  35.4 us (5%)
  local copies, waits for them, and re-layouts  21 us (3%)
  between operations  17.3 us (2%)
    reduce_scatter x1, waiting for transfers between devices, body(): lax.psum_scatter(lax.dot_general(columns, scaled_err, (((0,), (0,)), ((),...  235 us
    psum x1, waiting for transfers between devices, body(): lax.psum(partial_value.astype(jnp.bfloat16), 'tp').astype(jnp.float32)  105 us
    all_gather x1, waiting for transfers between devices, body(): lax.all_gather(draft_weight, 'req', axis=0, tiled=True)  90.7 us
    all_gather x1, waiting for transfers between devices, body(): full_residual = lax.all_gather(residual, 'tp', axis=2, tiled=True)  42.8 us
    psum x1, blocking collectives, body(): lax.psum((jnp.sum(gradient * gradient), jnp.sum(weights * pred_error * pr...  39.6 us
    pmax x1, blocking collectives, body(): row_top = lax.pmax(local_top, 'tp')  39.3 us
    unnamed x1, blocking collectives  33.4 us
    reduce_scatter x1, waiting for transfers between devices, body(): lax.psum_scatter(weighted, 'tp', scatter_dimension=1, tiled=True)  24.9 us
  transfers between devices with their start and end apart: 5, of which 5 were waited for; matrix products, arithmetic and copies ran while one was open for 4% of the time, Pallas kernels for 0%

commit v1 on v0

v1 whole, which is shorter than its diff:
```python
import functools
import math

import jax
import jax.numpy as jnp
from jax import lax
from jax.experimental import pallas as pl
from jax.experimental.pallas import tpu as pltpu
from jax.sharding import PartitionSpec as P

HEADS = 32
KV_HEADS = 4
HEAD = 128
NODES = 32
CACHE = 4096


NEG_FILL = -1e30
NORM_EPSILON = 1e-06
BETA_ONE = 0.9
BETA_TWO = 0.95
CORRECT_ONE = 1.0 - 0.9**10
CORRECT_TWO = 1.0 - 0.95**10
LEARN_RATE = 0.001


def closure(parents):
    node_count = parents.shape[-1]
    onehot = (parents[:, :, None] == jnp.arange(node_count, dtype=jnp.int32)[None, None, :]).astype(
        jnp.float32
    )
    reach_map = jnp.eye(node_count, dtype=jnp.float32)[None] + onehot
    for repeat in range(node_count.bit_length()):
        reach_map = jnp.minimum(
            jnp.einsum("rij,rjk->rik", reach_map, reach_map, precision=lax.Precision.HIGHEST), 1.0
        )
    return reach_map


VMEM = pl.BlockSpec(memory_space=pltpu.VMEM)
MESH = pl.DeviceIdType.MESH


def greet(axis, size):
    me = lax.axis_index(axis)
    barrier = pltpu.get_barrier_semaphore()
    for k in range(1, size):
        pl.semaphore_signal(
            barrier, inc=1, device_id={axis: lax.rem(me + k, size)}, device_id_type=MESH
        )
    pl.semaphore_wait(barrier, size - 1)


def params(cid):
    return pltpu.CompilerParams(
        collective_id=cid, has_side_effects=True, vmem_limit_bytes=40 * 1024 * 1024
    )


def exchange_kernel(axis, size, gather, count, *refs):
    ins, outs = refs[:count], refs[count : 2 * count]
    send_sem, recv_sem = refs[2 * count :]
    me = lax.axis_index(axis)
    greet(axis, size)
    copies = []
    for k in range(1, size):
        peer = lax.rem(me + k, size)
        for a in range(count):
            copy = pltpu.make_async_remote_copy(
                src_ref=ins[a] if gather else ins[a].at[peer],
                dst_ref=outs[a].at[me],
                send_sem=send_sem.at[a, k],
                recv_sem=recv_sem.at[a, k],
                device_id={axis: peer},
                device_id_type=MESH,
            )
            copy.start()
            copies.append(copy)
    for a in range(count):
        outs[a][me] = ins[a][...] if gather else ins[a][me]
    for copy in copies:
        copy.wait()


def exchange(arrays, axis, cid, gather=False):
    size = lax.axis_size(axis)
    count = len(arrays)
    shapes = [
        jax.ShapeDtypeStruct((size,) + a.shape if gather else a.shape, a.dtype) for a in arrays
    ]
    return pl.pallas_call(
        functools.partial(exchange_kernel, axis, size, gather, count),
        out_shape=shapes,
        in_specs=[VMEM] * count,
        out_specs=[VMEM] * count,
        scratch_shapes=[
            pltpu.SemaphoreType.DMA((count, size)),
            pltpu.SemaphoreType.DMA((count, size)),
        ],
        compiler_params=params(cid),
    )(*arrays)


def project_kernel(
    size, att, weight, residual, gain, out, parts, sent, squares, mine, mixed, sems
):
    me = lax.axis_index("tp")
    width = out.shape[1]
    model_width = width * size
    greet("tp", size)
    copies = []
    for k in range(1, size + 1):
        peer = lax.rem(me + k, size)
        columns = pl.ds(pl.multiple_of(peer * width, width), width)
        term = jnp.dot(att[...], weight[:, columns], preferred_element_type=jnp.float32)
        if k == size:
            parts[me] = term.astype(jnp.bfloat16)
        else:
            sent[peer] = term.astype(jnp.bfloat16)
            copy = pltpu.make_async_remote_copy(
                src_ref=sent.at[peer],
                dst_ref=parts.at[me],
                send_sem=sems.at[0, k],
                recv_sem=sems.at[1, k],
                device_id={"tp": peer},
                device_id_type=MESH,
            )
            copy.start()
            copies.append(copy)
    mixed[...] = residual[...].astype(jnp.float32) + parts[me].astype(jnp.float32)
    for k in range(1, size):
        copies[k - 1].wait()
        origin = lax.rem(me + size - k, size)
        mixed[...] += parts[origin].astype(jnp.float32)
    total = jnp.sum(mixed[...] * mixed[...], axis=1, keepdims=True)
    mine[...] = jnp.broadcast_to(total, mine.shape)
    copies = []
    for k in range(1, size):
        copy = pltpu.make_async_remote_copy(
            src_ref=mine,
            dst_ref=squares.at[me],
            send_sem=sems.at[2, k],
            recv_sem=sems.at[3, k],
            device_id={"tp": lax.rem(me + k, size)},
            device_id_type=MESH,
        )
        copy.start()
        copies.append(copy)
    squares[me] = mine[...]
    for copy in copies:
        copy.wait()
    total = jnp.sum(squares[...], axis=0)[:, 0:1] / model_width
    out[...] = (mixed[...] * lax.rsqrt(total + NORM_EPSILON) * gain[...]).astype(jnp.bfloat16)


def project(att, weight, residual, gain, cid):
    size = lax.axis_size("tp")
    rows, width = residual.shape
    return pl.pallas_call(
        functools.partial(project_kernel, size),
        out_shape=jax.ShapeDtypeStruct((rows, width), jnp.bfloat16),
        in_specs=[VMEM] * 4,
        out_specs=VMEM,
        scratch_shapes=[
            pltpu.VMEM((size, rows, width), jnp.bfloat16),
            pltpu.VMEM((size, rows, width), jnp.bfloat16),
            pltpu.VMEM((size, rows, 128), jnp.float32),
            pltpu.VMEM((rows, 128), jnp.float32),
            pltpu.VMEM((rows, width), jnp.float32),
            pltpu.SemaphoreType.DMA((4, size)),
        ],
        compiler_params=params(cid),
    )(att, weight, residual, gain)


def spread_kernel(reqs, tps, x_ref, out_ref, send_sem, recv_sem):
    per = tps // reqs
    r, t = lax.axis_index("req"), lax.axis_index("tp")
    goal, part = t // per, t % per
    own = r == goal
    barrier = pltpu.get_barrier_semaphore()

    def others(source, piece):
        return jnp.logical_or(r != source, t != r * per + piece)

    for source in range(reqs):
        for piece in range(per):

            @pl.when(others(source, piece))
            def _():
                pl.semaphore_signal(
                    barrier,
                    inc=1,
                    device_id={"req": source, "tp": r * per + piece},
                    device_id_type=MESH,
                )

    @pl.when(own)
    def _():
        pl.semaphore_wait(barrier, tps - 1)

    @pl.when(jnp.logical_not(own))
    def _():
        pl.semaphore_wait(barrier, tps)

    def send(k):
        return pltpu.make_async_remote_copy(
            src_ref=x_ref,
            dst_ref=out_ref.at[r, part],
            send_sem=send_sem.at[k],
            recv_sem=recv_sem.at[r * per + part],
            device_id={"req": goal, "tp": lax.rem(t + k, tps)},
            device_id_type=MESH,
        )

    for k in range(1, tps):
        send(k).start()

    @pl.when(jnp.logical_not(own))
    def _():
        send(0).start()

    @pl.when(own)
    def _():
        out_ref[r, part] = x_ref[...]

    for source in range(reqs):
        for piece in range(per):

            @pl.when(others(source, piece))
            def _():
                pltpu.make_async_remote_copy(
                    src_ref=x_ref,
                    dst_ref=out_ref.at[source, piece],
                    send_sem=send_sem.at[0],
                    recv_sem=recv_sem.at[source * per + piece],
                    device_id={"req": source, "tp": r * per + piece},
                    device_id_type=MESH,
                ).wait_recv()

    for k in range(1, tps):
        send(k).wait_send()

    @pl.when(jnp.logical_not(own))
    def _():
        send(0).wait_send()


def spread(x, cid):
    reqs, tps = lax.axis_size("req"), lax.axis_size("tp")
    return pl.pallas_call(
        functools.partial(spread_kernel, reqs, tps),
        out_shape=jax.ShapeDtypeStruct((reqs, tps // reqs) + x.shape, x.dtype),
        in_specs=[VMEM],
        out_specs=VMEM,
        scratch_shapes=[pltpu.SemaphoreType.DMA((tps,)), pltpu.SemaphoreType.DMA((tps,))],
        compiler_params=params(cid),
    )(x)


def body(
    queries,
    cache_keys,
    cache_values,
    tree_keys,
    tree_values,
    parents,
    lengths,
    accepted_leaf,
    residual,
    norm_gain,
    out_weight,
    prev_feature,
    draft_weight,
    first_moment,
    second_moment,
):
    requests = queries.shape[0]
    row_count = requests * NODES
    groups = HEADS // KV_HEADS
    score_scale = 1.0 / math.sqrt(HEAD)
    tps, reqs = lax.axis_size("tp"), lax.axis_size("req")
    tp_rank = lax.axis_index("tp")
    cache_span = cache_keys.shape[1]
    tree_span = tree_keys.shape[1]
    reach_map = closure(parents)
    query_view = queries.reshape(requests, NODES, KV_HEADS, groups, HEAD)
    cache_view = cache_keys.reshape(requests, cache_span, KV_HEADS, HEAD)
    tree_view = tree_keys.reshape(requests, tree_span, KV_HEADS, HEAD)
    cache_scores = (
        jnp.einsum("rnkgd,rckd->rkgnc", query_view, cache_view, preferred_element_type=jnp.float32)
        * score_scale
    )
    tree_scores = (
        jnp.einsum("rnkgd,rjkd->rkgnj", query_view, tree_view, preferred_element_type=jnp.float32)
        * score_scale
    )
    positions = tp_rank * cache_span + jnp.arange(cache_span, dtype=jnp.int32)
    cache_live = (positions[None, :] < lengths[:, None])[:, None, None, None, :]
    visible = lax.dynamic_slice_in_dim(reach_map, tp_rank * tree_span, tree_span, 2)
    tree_live = (visible > 0.5)[:, None, None, :, :]
    cache_scores = jnp.where(cache_live, cache_scores, NEG_FILL)
    tree_scores = jnp.where(tree_live, tree_scores, NEG_FILL)
    local_top = jnp.maximum(jnp.max(cache_scores, axis=-1), jnp.max(tree_scores, axis=-1))
    cache_probs = jnp.where(cache_live, jnp.exp(cache_scores - local_top[..., None]), 0.0).astype(
        jnp.bfloat16
    )
    tree_probs = jnp.where(tree_live, jnp.exp(tree_scores - local_top[..., None]), 0.0).astype(
        jnp.bfloat16
    )
    totals = jnp.sum(cache_probs, axis=-1, dtype=jnp.float32) + jnp.sum(
        tree_probs, axis=-1, dtype=jnp.float32
    )
    value_view = cache_values.reshape(requests, cache_span, KV_HEADS, HEAD)
    tree_value_view = tree_values.reshape(requests, tree_span, KV_HEADS, HEAD)
    weighted = jnp.einsum(
        "rkgnc,rckd->rkgnd", cache_probs, value_view, preferred_element_type=jnp.float32
    )
    weighted = weighted + jnp.einsum(
        "rkgnj,rjkd->rkgnd", tree_probs, tree_value_view, preferred_element_type=jnp.float32
    )
    own_heads = HEADS // tps
    weighted = weighted.astype(jnp.bfloat16).reshape(requests, tps, own_heads, NODES, HEAD)
    weighted = jnp.transpose(weighted, (1, 2, 0, 3, 4)).reshape(tps, own_heads * row_count, HEAD)

    def by_owner(x):
        x = x.reshape(requests, tps, own_heads, NODES)
        return jnp.transpose(x, (1, 2, 0, 3)).reshape(tps, own_heads, row_count)

    stats = jnp.concatenate([by_owner(local_top), by_owner(totals)], axis=1)
    weighted, stats = exchange([weighted, stats], "tp", 1)
    tops, totals = stats[:, :own_heads], stats[:, own_heads:]
    shares = jnp.exp(tops - jnp.max(tops, axis=0, keepdims=True))
    head_totals = jnp.sum(shares * totals, axis=0)
    shares = shares / head_totals[None]
    head_sums = jnp.sum(
        weighted.reshape(tps, own_heads, row_count, HEAD).astype(jnp.float32)
        * shares[:, :, :, None],
        axis=0,
    )
    attended = jnp.transpose(head_sums, (1, 0, 2)).reshape(row_count, own_heads * HEAD)
    attended = attended.astype(jnp.bfloat16)
    model_width = out_weight.shape[1]
    block_width = model_width // tps
    own_gain = lax.dynamic_slice_in_dim(norm_gain, tp_rank * block_width, block_width, 0)
    own_block = project(
        attended, out_weight, residual.reshape(row_count, block_width), own_gain[None, :], 2
    )
    own_prev = lax.dynamic_slice_in_dim(prev_feature, tp_rank * block_width, block_width, 1)
    node_hot = (parents[:, :, None] == jnp.arange(NODES, dtype=jnp.int32)[None, None, :]).astype(
        jnp.bfloat16
    )
    picked = jnp.einsum(
        "rij,rjd->rid",
        node_hot,
        own_block.reshape(requests, NODES, block_width),
        preferred_element_type=jnp.float32,
    )
    inputs = jnp.where(
        (parents < 0)[:, :, None], own_prev[:, None, :], picked.astype(jnp.bfloat16)
    ).reshape(row_count, block_width)
    leaf_hot = (accepted_leaf[:, None] == jnp.arange(NODES, dtype=jnp.int32)[None, :]).astype(
        jnp.float32
    )
    accepted = jnp.einsum("rn,rnj->rj", leaf_hot, reach_map, precision=lax.Precision.HIGHEST)
    fill_share = 0.5 + lengths.astype(jnp.float32) / CACHE
    weights = ((1.0 + 3.0 * accepted) * fill_share[:, None]).reshape(row_count, 1)
    all_inputs = spread(inputs, 3)
    per = tps // reqs
    all_inputs = [
        all_inputs[:, piece].reshape(reqs * row_count, block_width) for piece in range(per)
    ]
    terms = jnp.dot(
        all_inputs[0], draft_weight[:block_width], preferred_element_type=jnp.float32
    )
    for piece in range(1, per):
        terms = terms + jnp.dot(
            all_inputs[piece],
            draft_weight[piece * block_width : (piece + 1) * block_width],
            preferred_element_type=jnp.float32,
        )
    (terms,) = exchange(
        [terms.astype(jnp.bfloat16).reshape(reqs, row_count, block_width)], "req", 4
    )
    predicted = jnp.sum(terms.astype(jnp.float32), axis=0)
    pred_error = predicted - own_block.astype(jnp.float32)
    scaled_err = (weights * pred_error).astype(jnp.bfloat16)
    (all_err,) = exchange([scaled_err], "req", 5, gather=True)
    all_err = all_err.reshape(reqs * row_count, block_width)
    gradient = jnp.concatenate(
        [
            lax.dot_general(
                columns, all_err, (((0,), (0,)), ((), ())), preferred_element_type=jnp.float32
            )
            for columns in all_inputs
        ],
        axis=0,
    )
    sums = jnp.stack([jnp.sum(gradient * gradient), jnp.sum(weights * pred_error * pred_error)])
    sums = jnp.broadcast_to(jnp.repeat(sums, 4)[:, None], (8, 128))
    (sums,) = exchange([sums], "tp", 6, gather=True)
    (sums,) = exchange([jnp.sum(sums, axis=0)], "req", 7, gather=True)
    sums = jnp.sum(sums, axis=0)
    square_total, error_total = sums[0, 0], sums[4, 0]
    draft_loss = 0.5 * error_total / (row_count * reqs * model_width)
    grad_norm = jnp.sqrt(square_total) + 1e-06
    clip_factor = jnp.minimum(1.0, model_width / grad_norm)
    clipped = gradient * clip_factor
    new_first = BETA_ONE * first_moment + (1.0 - BETA_ONE) * clipped
    new_second = BETA_TWO * second_moment + (1.0 - BETA_TWO) * clipped * clipped
    direction = new_first / CORRECT_ONE / (jnp.sqrt(new_second / CORRECT_TWO) + 1e-08)
    new_weight = (draft_weight.astype(jnp.float32) - LEARN_RATE * direction).astype(jnp.bfloat16)
    return (
        own_block.reshape(requests, NODES, block_width),
        new_weight,
        new_first,
        new_second,
        draft_loss,
    )


def solution(mesh):
    placed = (
        P("req", None, None),
        P("req", "tp", None),
        P("req", "tp", None),
        P("req", "tp", None),
        P("req", "tp", None),
        P("req", None),
        P("req"),
        P("req"),
        P("req", None, "tp"),
        P(),
        P("tp", None),
        P("req", None),
        P("req", "tp"),
        P("req", "tp"),
        P("req", "tp"),
    )
    return jax.shard_map(
        body,
        mesh=mesh,
        in_specs=placed,
        out_specs=(P("req", None, "tp"), P("req", "tp"), P("req", "tp"), P("req", "tp"), P()),
        check_vma=False,
    )
```

time: 731 us -> 255 us (0.35)
  waiting for transfers between devices: 499 us -> 0 us
  Pallas kernels: 0 us -> 186 us
  blocking collectives: 112 us -> 0 us
  matrix products: 44.6 us -> 18.8 us
  between operations: 17.3 us -> 3.59 us
    reduce_scatter x2 -> x0, waiting for transfers between devices: 260 us -> none  [the longest x1 235 us: body(): lax.psum_scatter(lax.dot_general(columns, scaled_err, (((0,), (0,)), ((),...]
    pallas_call x0 -> x7, Pallas kernels: none -> 186 us  [the longest x5 78.5 us: exchange(): pl.pallas_call(functools.partial(exchange_kernel, axis, size, gather, cou...]
    all_gather x2 -> x0, waiting for transfers between devices: 133 us -> none  [the longest x1 90.7 us: body(): lax.all_gather(draft_weight, 'req', axis=0, tiled=True)]
    psum x1 -> x0, waiting for transfers between devices: 105 us -> none  [body(): lax.psum(partial_value.astype(jnp.bfloat16), 'tp').astype(jnp.float32)]
    psum x1 -> x0, blocking collectives: 39.6 us -> none  [body(): lax.psum((jnp.sum(gradient * gradient), jnp.sum(weights * pred_error * pr...]
    pmax x1 -> x0, blocking collectives: 39.3 us -> none  [body(): row_top = lax.pmax(local_top, 'tp')]
    unnamed x1 -> x0, blocking collectives: 33.4 us -> none
    dot_general x5 -> x7, matrix products: 34.1 us -> 11 us  [the longest x1 5.1 us: body(): jnp.einsum('rkgnc,rckd->rkgnd', cache_probs, value_view, preferred_elemen...]
  transfers between devices with their start and end apart: 5 -> 0, of which waited for: 5 -> 0; matrix products, arithmetic and copies ran while one was open for 4% -> 0% of each run, Pallas kernels for 0% -> 0%
where the time goes in v1:
time: 255 us; the launch traced here: 254 us
  Pallas kernels  186 us (73%)
  other arithmetic  31 us (12%)
  matrix products  18.8 us (7%)
  local copies, waits for them, and re-layouts  14.5 us (6%)
  between operations  3.59 us (1%)
    pallas_call x5, Pallas kernels, exchange(): pl.pallas_call(functools.partial(exchange_kernel, axis, size, gather, cou...  78.5 us
    pallas_call x1, Pallas kernels, project(): pl.pallas_call(functools.partial(project_kernel, size), out_shape=jax.Sha...  69.2 us
    pallas_call x1, Pallas kernels, spread(): pl.pallas_call(functools.partial(spread_kernel, reqs, tps), out_shape=jax...  38.5 us
    convert_element_type x1, other arithmetic, body(): (draft_weight.astype(jnp.float32) - LEARN_RATE * direction).astype(jnp.bf...  19.3 us
    unnamed x29, local copies, waits for them, and re-layouts  6.38 us
    dot_general x1, matrix products, body(): jnp.einsum('rkgnc,rckd->rkgnd', cache_probs, value_view, preferred_elemen...  5.1 us

profile of v1, /device:TPU:0, one launch (start us, length us, event | category | flops | bytes accessed | tf_op | source)
XLA Modules:
  0.0 254.2 jit_solution(3281936191609201393)
XLA Ops:
  0.7 0.9 fusion.33
  4.3 1.1 convolution_minimum_fusion.5
  6.8 1.5 copy.101
  8.2 2.2 fusion.38
  10.5 4.0 %reshape.129 = bf16[4,512,4,128]{3,2,1,0:T(4,128)(2,1)} reshape(bf16[4,512,512]{2,1,0:T(8,128)(2,1)} %param.16) | data formatting | bytes 4194304 | tf_op jit(solution)/shard_map/reshape | solution.py:288
  14.4 2.0 reshape.132
  16.4 3.4 %bitcast_reduce_fusion = (f32[4,4,8,32]{3,2,1,0:T(8,128)S(1)}, f32[4,4,512,32,8]{2,3,4,1,0:T(8,128)S(1)}) fusion(pred[4,512]{1,0:T(4,128)(4,1)S(1)} %broadcast_compare_fusion, bf16[4,32,4,8,128]{4,3,2,1,0:T(8,128)(2,1)S(1)} %bitcast.115, bf16[4,512,4,128,1]{3,2,1,0,4:T(4,128)(2,1)} %bitcast.112), kind=kOutput, calls=%fused_computation.4 | convolution fusion | flops 543158272 | bytes 11552768 | tf_op jit(solution)/shard_map/rnkgd,rckd->rkgnc/dot_general | solution.py:291
  19.8 3.5 %copy-done.5 = f32[4,4,512,32,8]{2,3,4,1,0:T(8,128)} copy-done((f32[4,4,512,32,8]{2,3,4,1,0:T(8,128)}, f32[4,4,512,32,8]{2,3,4,1,0:T(8,128)S(1)}, u32[]{:S(2)}) %copy-start.5) | copy-done | bytes 8388632
  23.3 2.4 convert_reduce_fusion
  26.9 5.1 %add_convert_fusion.1 = bf16[4,4,8,32,128]{4,3,2,1,0:T(8,128)(2,1)S(1)} fusion(f32[4,4,8,32,128]{4,3,2,1,0:T(8,128)S(1)} %fusion.27, bf16[4,512,4,128,1]{3,2,1,0,4:T(4,128)(2,1)S(1)} %bitcast.111, f32[4,4,512,32,8]{2,3,4,1,0:T(8,128)} %copy-done.5, f32[4,4,8,32]{3,2,1,0:T(8,128)S(1)} %max.11, pred[4,512]{1,0:T(4,128)(4,1)S(1)} %broadcast_compare_fusion), kind=kOutput, calls=%fused_computation.24 | convolution fusion | flops 548405248 | bytes 13649920 | tf_op jit(solution)/shard_map/rkgnc,rckd->rkgnd/dot_general | solution.py:316
  32.2 23.7 %shard_map.182 = (bf16[8,512,128]{2,1,0:T(8,128)(2,1)S(1)}, f32[8,8,128]{2,1,0:T(8,128)S(1)}) custom-call(bf16[8,512,128]{2,1,0:T(8,128)(2,1)S(1)} %bitcast.101, f32[8,8,128]{2,1,0:T(8,128)S(1)} %pad_maximum_fusion.1.refs_1_), custom_call_target="tpu_custom_call" | custom-call | tf_op jit(solution)/shard_map/pallas_call | solution.py:91
  56.7 69.2 %shard_map.183 = bf16[128,1024]{1,0:T(8,128)(2,1)S(1)} custom-call(bf16[128,512]{1,0:T(8,128)(2,1)S(1)} %bitcast.104, bf16[512,8192]{1,0:T(8,128)(2,1)S(1)} %bitcast.98, bf16[128,1024]{1,0:T(8,128)(2,1)S(1)} %bitcast.105, f32[1,1024]{1,0:T(1,128)S(1)} %bitcast.106), custom_call_target="tpu_custom_call" | custom-call | tf_op jit(solution)/shard_map/pallas_call | solution.py:159
  126.2 38.5 %shard_map.184 = bf16[4,2,128,1024]{3,2,1,0:T(8,128)(2,1)S(1)} custom-call(bf16[128,1024]{1,0:T(8,128)(2,1)S(1)} %bitcast.102), custom_call_target="tpu_custom_call" | custom-call | tf_op jit(solution)/shard_map/pallas_call | solution.py:251
  165.0 1.3 fusion.8
  166.3 1.3 add_convert_fusion
  167.6 27.9 %shard_map.185 = bf16[4,128,1024]{2,1,0:T(8,128)(2,1)S(1)} custom-call(bf16[4,128,1024]{2,1,0:T(8,128)(2,1)S(1)} %bitcast.103), custom_call_target="tpu_custom_call" | custom-call | tf_op jit(solution)/shard_map/pallas_call | solution.py:91
  196.5 13.8 %shard_map.186 = bf16[4,128,1024]{2,1,0:T(8,128)(2,1)S(1)} custom-call(bf16[128,1024]{1,0:T(8,128)(2,1)S(1)} %get-tuple-element.14.refs_0_), custom_call_target="tpu_custom_call" | custom-call | tf_op jit(solution)/shard_map/pallas_call | solution.py:91
  210.3 1.3 fusion.40
  211.6 1.3 fusion.39
  213.5 2.8 %multiply_reduce_fusion = f32[]{:T(128)} fusion(f32[1024,1024]{1,0:T(8,128)S(1)} %fusion.40, f32[1024,1024]{1,0:T(8,128)S(1)} %fusion.39), kind=kLoop, calls=%fused_computation.10 | loop fusion | flops 6291455 | bytes 8388612 | tf_op jit(solution)/shard_map/reduce_sum | solution.py:399
  216.3 1.4 pad_maximum_fusion.2
  217.9 9.4 %shard_map.187 = f32[8,8,128]{2,1,0:T(8,128)S(1)} custom-call(f32[8,128]{1,0:T(8,128)S(1)} %broadcast_in_dim.98.refs_0_), custom_call_target="tpu_custom_call" | custom-call | tf_op jit(solution)/shard_map/pallas_call | solution.py:91
  227.3 3.7 %shard_map.188 = f32[4,8,128]{2,1,0:T(8,128)S(1)} custom-call(f32[8,128]{1,0:T(8,128)S(1)} %reduce_sum.88.refs_0_), custom_call_target="tpu_custom_call" | custom-call | tf_op jit(solution)/shard_map/pallas_call | solution.py:91
  233.0 19.3 %subtract_convert_fusion = (bf16[2048,1024]{1,0:T(8,128)(2,1)}, f32[2048,1024]{1,0:T(8,128)}, f32[2048,1024]{1,0:T(8,128)}) fusion(bf16[2048,1024]{1,0:T(8,128)(2,1)} %param.27, f32[]{:T(128)} %bitcast.32, f32[1024,1024]{1,0:T(8,128)} %copy-done.3, f32[1024,1024]{1,0:T(8,128)} %copy-done.4, f32[2048,1024]{1,0:T(8,128)} %param.28, f32[2048,1024]{1,0:T(8,128)} %param.29), kind=kLoop, calls=%fused_computation.8 | loop fusion | flops 35651584 | bytes 50331652 | tf_op jit(solution)/shard_map/convert_element_type | solution.py:412
  (69 shorter events, 9.7 us)
Async XLA Ops:
  0.6 3.7 %copy-start = (bf16[4,8192]{1,0:T(4,128)(2,1)S(1)}, bf16[4,8192]{1,0:T(4,128)(2,1)}, u32[]{:S(2)}) copy-start(bf16[4,8192]{1,0:T(4,128)(2,1)} %param.26) | copy-start | bytes 196612
  0.6 13.8 %copy-start.7 = (bf16[4,512,512]{2,1,0:T(8,128)(2,1)S(1)}, bf16[4,512,512]{2,1,0:T(8,128)(2,1)}, u32[]{:S(2)}) copy-start(bf16[4,512,512]{2,1,0:T(8,128)(2,1)} %param.17) | copy-start | bytes 6291460
  16.4 9.9 %copy-start.10 = (bf16[4,4,512]{2,1,0:T(4,128)(2,1)S(1)}, bf16[4,4,512]{2,1,0:T(4,128)(2,1)}, u32[]{:S(2)}) copy-start(bf16[4,4,512]{2,1,0:T(4,128)(2,1)} %param.19) | copy-start | bytes 49156
  19.8 3.5 %copy-start.5 = (f32[4,4,512,32,8]{2,3,4,1,0:T(8,128)}, f32[4,4,512,32,8]{2,3,4,1,0:T(8,128)S(1)}, u32[]{:S(2)}) copy-start(f32[4,4,512,32,8]{2,3,4,1,0:T(8,128)S(1)} %get-tuple-element.19) | copy-start | bytes 25165828
  19.8 7.1 %copy-start.8 = (bf16[4,512,4,128]{3,2,1,0:T(4,128)(2,1)S(1)}, bf16[4,512,4,128]{3,2,1,0:T(4,128)(2,1)}, u32[]{:S(2)}) copy-start(bf16[4,512,4,128]{3,2,1,0:T(4,128)(2,1)} %reshape.132) | copy-start | bytes 6291460
  26.3 30.4 %slice-start = ((s8[8388608]{0:T(1024)(128)(4,1)}), s8[4194304]{0:T(1024)(128)(4,1)S(1)}, s32[]{:S(2)}) async-start(s8[8388608]{0:T(1024)(128)(4,1)} %bitcast.97), calls=%async_computation | async-start | bytes 8388608
  26.9 29.8 %slice-start.1 = ((s8[8388608]{0:T(1024)(128)(4,1)}), s8[4194304]{0:T(1024)(128)(4,1)S(1)}, s32[]{:S(2)}) async-start(s8[8388608]{0:T(1024)(128)(4,1)} %bitcast.97), calls=%async_computation.1 | async-start | bytes 8388608
  26.9 29.8 %copy-start.2 = (bf16[4,32,1024]{2,1,0:T(8,128)(2,1)S(1)}, bf16[4,32,1024]{2,1,0:T(8,128)(2,1)}, u32[]{:S(2)}) copy-start(bf16[4,32,1024]{2,1,0:T(8,128)(2,1)} %param.23) | copy-start | bytes 786436
  32.0 93.9 %copy-start.9 = (s32[4,32]{1,0:T(4,128)S(1)}, s32[4,32]{1,0:T(4,128)}, u32[]{:S(2)}) copy-start(s32[4,32]{1,0:T(4,128)} %param.20) | copy-start | bytes 1540
  56.7 108.3 %copy-start.6 = (bf16[2048,1024]{1,0:T(8,128)(2,1)S(1)}, bf16[2048,1024]{1,0:T(8,128)(2,1)}, u32[]{:S(2)}) copy-start(bf16[2048,1024]{1,0:T(8,128)(2,1)} %param.27) | copy-start | bytes 12582916
  211.6 1.9 copy-start.3
  213.5 2.8 %copy-start.4 = (f32[1024,1024]{1,0:T(8,128)}, f32[1024,1024]{1,0:T(8,128)S(1)}, u32[]{:S(2)}) copy-start(f32[1024,1024]{1,0:T(8,128)S(1)} %fusion.39) | copy-start | bytes 12582916
  233.0 20.1 %copy-start.1 = (bf16[4,8192]{1,0:T(4,128)(2,1)S(1)}, bf16[4,8192]{1,0:T(4,128)(2,1)}, u32[]{:S(2)}) copy-start(bf16[4,8192]{1,0:T(4,128)(2,1)} %param.26) | copy-start | bytes 196612

commit v2 on v1

--- a/solution.py
+++ b/solution.py
@@ -102,45 +102,75 @@
 
 
 def project_kernel(
-    size, att, weight, residual, gain, out, parts, sent, squares, mine, mixed, sems
+    size, att, weight, residual, gain, out, parts, sent, sums, passed, squares, mine, mixed, near, far, small
 ):
     me = lax.axis_index("tp")
     width = out.shape[1]
     model_width = width * size
+    zs, xs = 4, size // 4
+    z, x = me // xs, me % xs
     greet("tp", size)
-    copies = []
-    for k in range(1, size + 1):
-        peer = lax.rem(me + k, size)
-        columns = pl.ds(pl.multiple_of(peer * width, width), width)
-        term = jnp.dot(att[...], weight[:, columns], preferred_element_type=jnp.float32)
-        if k == size:
-            parts[me] = term.astype(jnp.bfloat16)
+
+    def to_x(step, k):
+        goal, other = lax.rem(z + step, zs), lax.rem(x + k, xs)
+        return pltpu.make_async_remote_copy(
+            src_ref=sent.at[goal, other],
+            dst_ref=parts.at[goal, x],
+            send_sem=near.at[0, step, k],
+            recv_sem=near.at[1, step, k],
+            device_id={"tp": z * xs + other},
+            device_id_type=MESH,
+        )
+
+    def to_z(step):
+        goal = lax.rem(z + step, zs)
+        return pltpu.make_async_remote_copy(
+            src_ref=passed.at[goal],
+            dst_ref=sums.at[z],
+            send_sem=far.at[0, step],
+            recv_sem=far.at[1, step],
+            device_id={"tp": goal * xs + x},
+            device_id_type=MESH,
+        )
+
+    steps = [*range(1, zs), 0]
+    for step in steps:
+        goal = lax.rem(z + step, zs)
+        for k in [*range(1, xs), 0]:
+            other = lax.rem(x + k, xs)
+            peer = goal * xs + other
+            columns = pl.ds(pl.multiple_of(peer * width, width), width)
+            term = jnp.dot(att[...], weight[:, columns], preferred_element_type=jnp.float32)
+            term = term.astype(jnp.bfloat16)
+            if k == 0:
+                parts[goal, x] = term
+            else:
+                sent[goal, other] = term
+                to_x(step, k).start()
+    for step in steps:
+        goal = lax.rem(z + step, zs)
+        total = parts[goal, x].astype(jnp.float32)
+        for k in range(1, xs):
+            to_x(step, k).wait()
+            total = total + parts[goal, lax.rem(x + xs - k, xs)].astype(jnp.float32)
+        if step == 0:
+            mixed[...] = residual[...].astype(jnp.float32) + total
         else:
-            sent[peer] = term.astype(jnp.bfloat16)
-            copy = pltpu.make_async_remote_copy(
-                src_ref=sent.at[peer],
-                dst_ref=parts.at[me],
-                send_sem=sems.at[0, k],
-                recv_sem=sems.at[1, k],
-                device_id={"tp": peer},
-                device_id_type=MESH,
-            )
-            copy.start()
-            copies.append(copy)
-    mixed[...] = residual[...].astype(jnp.float32) + parts[me].astype(jnp.float32)
-    for k in range(1, size):
-        copies[k - 1].wait()
-        origin = lax.rem(me + size - k, size)
-        mixed[...] += parts[origin].astype(jnp.float32)
+            passed[goal] = total.astype(jnp.bfloat16)
+            to_z(step).start()
+    for step in range(1, zs):
+        to_z(step).wait()
+        mixed[...] += sums[lax.rem(z + zs - step, zs)].astype(jnp.float32)
+    rows = mixed.shape[0]
     total = jnp.sum(mixed[...] * mixed[...], axis=1, keepdims=True)
-    mine[...] = jnp.broadcast_to(total, mine.shape)
+    mine[...] = jnp.transpose(jnp.broadcast_to(total, (rows, 128)))[0:8]
     copies = []
     for k in range(1, size):
         copy = pltpu.make_async_remote_copy(
             src_ref=mine,
             dst_ref=squares.at[me],
-            send_sem=sems.at[2, k],
-            recv_sem=sems.at[3, k],
+            send_sem=small.at[0, k],
+            recv_sem=small.at[1, k],
             device_id={"tp": lax.rem(me + k, size)},
             device_id_type=MESH,
         )
@@ -149,7 +179,8 @@
     squares[me] = mine[...]
     for copy in copies:
         copy.wait()
-    total = jnp.sum(squares[...], axis=0)[:, 0:1] / model_width
+    total = jnp.sum(squares[...], axis=0)[0:1]
+    total = jnp.transpose(jnp.broadcast_to(total, (128, rows)))[:, 0:1] / model_width
     out[...] = (mixed[...] * lax.rsqrt(total + NORM_EPSILON) * gain[...]).astype(jnp.bfloat16)
 
 
@@ -162,46 +193,63 @@
         in_specs=[VMEM] * 4,
         out_specs=VMEM,
         scratch_shapes=[
-            pltpu.VMEM((size, rows, width), jnp.bfloat16),
-            pltpu.VMEM((size, rows, width), jnp.bfloat16),
-            pltpu.VMEM((size, rows, 128), jnp.float32),
-            pltpu.VMEM((rows, 128), jnp.float32),
+            pltpu.VMEM((4, size // 4, rows, width), jnp.bfloat16),
+            pltpu.VMEM((4, size // 4, rows, width), jnp.bfloat16),
+            pltpu.VMEM((4, rows, width), jnp.bfloat16),
+            pltpu.VMEM((4, rows, width), jnp.bfloat16),
+            pltpu.VMEM((size, 8, rows), jnp.float32),
+            pltpu.VMEM((8, rows), jnp.float32),
             pltpu.VMEM((rows, width), jnp.float32),
-            pltpu.SemaphoreType.DMA((4, size)),
+            pltpu.SemaphoreType.DMA((2, 4, size // 4)),
+            pltpu.SemaphoreType.DMA((2, 4)),
+            pltpu.SemaphoreType.DMA((2, size)),
         ],
         compiler_params=params(cid),
     )(att, weight, residual, gain)
 
 
-def spread_kernel(reqs, tps, x_ref, out_ref, send_sem, recv_sem):
+def spread_kernel(reqs, tps, x_ref, out_ref, send_sem, recv_sem, pass_sem):
     per = tps // reqs
+    zs, xs = 4, tps // 4
     r, t = lax.axis_index("req"), lax.axis_index("tp")
+    z, x = t // xs, t % xs
     goal, part = t // per, t % per
     own = r == goal
+    blocks = [(source, piece) for source in range(reqs) for piece in range(per)]
     barrier = pltpu.get_barrier_semaphore()
+
+    def direct(piece):
+        return (r * per + piece) % xs == x
 
     def others(source, piece):
         return jnp.logical_or(r != source, t != r * per + piece)
 
-    for source in range(reqs):
-        for piece in range(per):
-
-            @pl.when(others(source, piece))
-            def _():
-                pl.semaphore_signal(
-                    barrier,
-                    inc=1,
-                    device_id={"req": source, "tp": r * per + piece},
-                    device_id_type=MESH,
-                )
+    for source, piece in blocks:
+
+        @pl.when(jnp.logical_and(direct(piece), others(source, piece)))
+        def _():
+            pl.semaphore_signal(
+                barrier,
+                inc=1,
+                device_id={"req": source, "tp": r * per + piece},
+                device_id_type=MESH,
+            )
+
+    for k in range(1, xs):
+        pl.semaphore_signal(
+            barrier,
+            inc=1,
+            device_id={"req": r, "tp": z * xs + lax.rem(x + k, xs)},
+            device_id_type=MESH,
+        )
 
     @pl.when(own)
     def _():
-        pl.semaphore_wait(barrier, tps - 1)
+        pl.semaphore_wait(barrier, zs + xs - 2)
 
     @pl.when(jnp.logical_not(own))
     def _():
-        pl.semaphore_wait(barrier, tps)
+        pl.semaphore_wait(barrier, zs + xs - 1)
 
     def send(k):
         return pltpu.make_async_remote_copy(
@@ -209,36 +257,54 @@
             dst_ref=out_ref.at[r, part],
             send_sem=send_sem.at[k],
             recv_sem=recv_sem.at[r * per + part],
-            device_id={"req": goal, "tp": lax.rem(t + k, tps)},
+            device_id={"req": goal, "tp": lax.rem(z + k, zs) * xs + x},
             device_id_type=MESH,
         )
 
-    for k in range(1, tps):
-        send(k).start()
+    def forward(source, piece, k):
+        return pltpu.make_async_remote_copy(
+            src_ref=out_ref.at[source, piece],
+            dst_ref=out_ref.at[source, piece],
+            send_sem=pass_sem.at[source * per + piece, k],
+            recv_sem=recv_sem.at[source * per + piece],
+            device_id={"req": r, "tp": z * xs + lax.rem(x + k, xs)},
+            device_id_type=MESH,
+        )
+
+    @pl.when(own)
+    def _():
+        out_ref[r, part] = x_ref[...]
 
     @pl.when(jnp.logical_not(own))
     def _():
         send(0).start()
 
-    @pl.when(own)
-    def _():
-        out_ref[r, part] = x_ref[...]
-
-    for source in range(reqs):
-        for piece in range(per):
-
+    for k in range(1, zs):
+        send(k).start()
+
+    for source, piece in blocks:
+
+        @pl.when(direct(piece))
+        def _():
             @pl.when(others(source, piece))
             def _():
-                pltpu.make_async_remote_copy(
-                    src_ref=x_ref,
-                    dst_ref=out_ref.at[source, piece],
-                    send_sem=send_sem.at[0],
-                    recv_sem=recv_sem.at[source * per + piece],
-                    device_id={"req": source, "tp": r * per + piece},
-                    device_id_type=MESH,
-                ).wait_recv()
-
-    for k in range(1, tps):
+                forward(source, piece, 1).wait_recv()
+
+            for k in range(1, xs):
+                forward(source, piece, k).start()
+
+    for source, piece in blocks:
+
+        @pl.when(direct(piece))
+        def _():
+            for k in range(1, xs):
+                forward(source, piece, k).wait_send()
+
+        @pl.when(jnp.logical_not(direct(piece)))
+        def _():
+            forward(source, piece, 1).wait_recv()
+
+    for k in range(1, zs):
         send(k).wait_send()
 
     @pl.when(jnp.logical_not(own))
@@ -253,7 +319,11 @@
         out_shape=jax.ShapeDtypeStruct((reqs, tps // reqs) + x.shape, x.dtype),
         in_specs=[VMEM],
         out_specs=VMEM,
-        scratch_shapes=[pltpu.SemaphoreType.DMA((tps,)), pltpu.SemaphoreType.DMA((tps,))],
+        scratch_shapes=[
+            pltpu.SemaphoreType.DMA((4,)),
+            pltpu.SemaphoreType.DMA((tps,)),
+            pltpu.SemaphoreType.DMA((tps, tps // 4)),
+        ],
         compiler_params=params(cid),
     )(x)
 

time: 255 us -> 218 us (0.85)
  Pallas kernels: 186 us -> 150 us
    pallas_call x1, Pallas kernels: 69.2 us -> 45.9 us  [project(): pl.pallas_call(functools.partial(project_kernel, size), out_shape=jax.Sha...]
    pallas_call x1, Pallas kernels: 38.5 us -> 22.4 us  [spread(): pl.pallas_call(functools.partial(spread_kernel, reqs, tps), out_shape=jax...]
    pallas_call x5, Pallas kernels: 78.5 us -> 81.6 us  [exchange(): pl.pallas_call(functools.partial(exchange_kernel, axis, size, gather, cou...]
where the time goes in v2:
time: 218 us
  Pallas kernels  150 us (69%)
  other arithmetic  31 us (14%)
  matrix products  18.8 us (9%)
  local copies, waits for them, and re-layouts  14.5 us (7%)
  between operations  3.59 us (2%)
    pallas_call x5, Pallas kernels, exchange(): pl.pallas_call(functools.partial(exchange_kernel, axis, size, gather, cou...  81.6 us
    pallas_call x1, Pallas kernels, project(): pl.pallas_call(functools.partial(project_kernel, size), out_shape=jax.Sha...  45.9 us
    pallas_call x1, Pallas kernels, spread(): pl.pallas_call(functools.partial(spread_kernel, reqs, tps), out_shape=jax...  22.4 us
    convert_element_type x1, other arithmetic, body(): (draft_weight.astype(jnp.float32) - LEARN_RATE * direction).astype(jnp.bf...  19.3 us
    unnamed x29, local copies, waits for them, and re-layouts  6.38 us
    dot_general x1, matrix products, body(): jnp.einsum('rkgnc,rckd->rkgnd', cache_probs, value_view, preferred_elemen...  5.1 us

profile of v2, /device:TPU:0, one launch (start us, length us, event | category | flops | bytes accessed | tf_op | source)
XLA Modules:
  0.0 217.8 jit_solution(8488211804318135093)
XLA Ops:
  0.7 0.9 fusion.33
  4.3 1.1 convolution_minimum_fusion.5
  6.8 1.5 copy.101
  8.2 2.2 %fusion.38 = (f32[4,4,8,32]{3,2,1,0:T(8,128)S(1)}, f32[4,4,8,32,4]{3,4,2,1,0:T(4,128)S(1)}) fusion(bf16[4,32,4,8,128]{4,3,2,1,0:T(8,128)(2,1)S(1)} %bitcast.114, bf16[4,4,512]{2,1,0:T(4,128)(2,1)} %param.18, pred[4,32,4]{1,2,0:T(4,128)(4,1)S(1)} %dynamic-slice_compare_fusion), kind=kOutput, calls=%fused_computation.77 | convolution fusion | flops 4239360 | bytes 1147392 | tf_op jit(solution)/shard_map/rnkgd,rjkd->rkgnj/dot_general | solution.py:365
  10.5 4.0 %reshape.129 = bf16[4,512,4,128]{3,2,1,0:T(4,128)(2,1)} reshape(bf16[4,512,512]{2,1,0:T(8,128)(2,1)} %param.16) | data formatting | bytes 4194304 | tf_op jit(solution)/shard_map/reshape | solution.py:358
  14.4 2.0 reshape.132
  16.4 3.4 %bitcast_reduce_fusion = (f32[4,4,8,32]{3,2,1,0:T(8,128)S(1)}, f32[4,4,512,32,8]{2,3,4,1,0:T(8,128)S(1)}) fusion(pred[4,512]{1,0:T(4,128)(4,1)S(1)} %broadcast_compare_fusion, bf16[4,32,4,8,128]{4,3,2,1,0:T(8,128)(2,1)S(1)} %bitcast.115, bf16[4,512,4,128,1]{3,2,1,0,4:T(4,128)(2,1)} %bitcast.112), kind=kOutput, calls=%fused_computation.4 | convolution fusion | flops 543158272 | bytes 11552768 | tf_op jit(solution)/shard_map/rnkgd,rckd->rkgnc/dot_general | solution.py:361
  19.8 3.5 %copy-done.5 = f32[4,4,512,32,8]{2,3,4,1,0:T(8,128)} copy-done((f32[4,4,512,32,8]{2,3,4,1,0:T(8,128)}, f32[4,4,512,32,8]{2,3,4,1,0:T(8,128)S(1)}, u32[]{:S(2)}) %copy-start.5) | copy-done | bytes 8388632
  23.3 2.4 %convert_reduce_fusion = f32[4,4,8,32]{3,2,1,0:T(8,128)S(1)} fusion(f32[4,4,8,32]{3,2,1,0:T(8,128)S(1)} %max.11, f32[4,4,512,32,8]{2,3,4,1,0:T(8,128)S(1)} %get-tuple-element.19, pred[4,512]{1,0:T(4,128)(4,1)S(1)} %broadcast_compare_fusion), kind=kLoop, calls=%fused_computation.11 | loop fusion | flops 14675968 | bytes 8423424 | tf_op jit(solution)/shard_map/reduce_sum | solution.py:381
  26.9 5.1 %add_convert_fusion.1 = bf16[4,4,8,32,128]{4,3,2,1,0:T(8,128)(2,1)S(1)} fusion(f32[4,4,8,32,128]{4,3,2,1,0:T(8,128)S(1)} %fusion.27, bf16[4,512,4,128,1]{3,2,1,0,4:T(4,128)(2,1)S(1)} %bitcast.111, f32[4,4,512,32,8]{2,3,4,1,0:T(8,128)} %copy-done.5, f32[4,4,8,32]{3,2,1,0:T(8,128)S(1)} %max.11, pred[4,512]{1,0:T(4,128)(4,1)S(1)} %broadcast_compare_fusion), kind=kOutput, calls=%fused_computation.24 | convolution fusion | flops 548405248 | bytes 13649920 | tf_op jit(solution)/shard_map/rkgnc,rckd->rkgnd/dot_general | solution.py:386
  32.2 23.7 %shard_map.182 = (bf16[8,512,128]{2,1,0:T(8,128)(2,1)S(1)}, f32[8,8,128]{2,1,0:T(8,128)S(1)}) custom-call(bf16[8,512,128]{2,1,0:T(8,128)(2,1)S(1)} %bitcast.101, f32[8,8,128]{2,1,0:T(8,128)S(1)} %pad_maximum_fusion.1.refs_1_), custom_call_target="tpu_custom_call" | custom-call | tf_op jit(solution)/shard_map/pallas_call | solution.py:91
  56.7 45.9 %shard_map.183 = bf16[128,1024]{1,0:T(8,128)(2,1)S(1)} custom-call(bf16[128,512]{1,0:T(8,128)(2,1)S(1)} %bitcast.104, bf16[512,8192]{1,0:T(8,128)(2,1)S(1)} %bitcast.98, bf16[128,1024]{1,0:T(8,128)(2,1)S(1)} %bitcast.105, f32[1,1024]{1,0:T(1,128)S(1)} %bitcast.106), custom_call_target="tpu_custom_call" | custom-call | tf_op jit(solution)/shard_map/pallas_call | solution.py:190
  102.9 22.4 %shard_map.184 = bf16[4,2,128,1024]{3,2,1,0:T(8,128)(2,1)S(1)} custom-call(bf16[128,1024]{1,0:T(8,128)(2,1)S(1)} %bitcast.102), custom_call_target="tpu_custom_call" | custom-call | tf_op jit(solution)/shard_map/pallas_call | solution.py:317
  125.5 1.3 fusion.8
  126.8 1.3 add_convert_fusion
  128.1 24.5 %shard_map.185 = bf16[4,128,1024]{2,1,0:T(8,128)(2,1)S(1)} custom-call(bf16[4,128,1024]{2,1,0:T(8,128)(2,1)S(1)} %bitcast.103), custom_call_target="tpu_custom_call" | custom-call | tf_op jit(solution)/shard_map/pallas_call | solution.py:91
  153.7 13.8 %shard_map.186 = bf16[4,128,1024]{2,1,0:T(8,128)(2,1)S(1)} custom-call(bf16[128,1024]{1,0:T(8,128)(2,1)S(1)} %get-tuple-element.14.refs_0_), custom_call_target="tpu_custom_call" | custom-call | tf_op jit(solution)/shard_map/pallas_call | solution.py:91
  167.4 1.3 fusion.40
  168.7 1.3 fusion.39
  170.6 2.8 %multiply_reduce_fusion = f32[]{:T(128)} fusion(f32[1024,1024]{1,0:T(8,128)S(1)} %fusion.40, f32[1024,1024]{1,0:T(8,128)S(1)} %fusion.39), kind=kLoop, calls=%fused_computation.10 | loop fusion | flops 6291455 | bytes 8388612 | tf_op jit(solution)/shard_map/reduce_sum | solution.py:469
  173.4 1.4 pad_maximum_fusion.2
  175.0 15.5 %shard_map.187 = f32[8,8,128]{2,1,0:T(8,128)S(1)} custom-call(f32[8,128]{1,0:T(8,128)S(1)} %broadcast_in_dim.98.refs_0_), custom_call_target="tpu_custom_call" | custom-call | tf_op jit(solution)/shard_map/pallas_call | solution.py:91
  190.5 4.2 %shard_map.188 = f32[4,8,128]{2,1,0:T(8,128)S(1)} custom-call(f32[8,128]{1,0:T(8,128)S(1)} %reduce_sum.88.refs_0_), custom_call_target="tpu_custom_call" | custom-call | tf_op jit(solution)/shard_map/pallas_call | solution.py:91
  196.7 19.3 %subtract_convert_fusion = (bf16[2048,1024]{1,0:T(8,128)(2,1)}, f32[2048,1024]{1,0:T(8,128)}, f32[2048,1024]{1,0:T(8,128)}) fusion(bf16[2048,1024]{1,0:T(8,128)(2,1)} %param.27, f32[]{:T(128)} %bitcast.32, f32[1024,1024]{1,0:T(8,128)} %copy-done.3, f32[1024,1024]{1,0:T(8,128)} %copy-done.4, f32[2048,1024]{1,0:T(8,128)} %param.28, f32[2048,1024]{1,0:T(8,128)} %param.29), kind=kLoop, calls=%fused_computation.8 | loop fusion | flops 35651584 | bytes 50331652 | tf_op jit(solution)/shard_map/convert_element_type | solution.py:482
  (69 shorter events, 9.7 us)
Async XLA Ops:
  0.6 3.7 %copy-start = (bf16[4,8192]{1,0:T(4,128)(2,1)S(1)}, bf16[4,8192]{1,0:T(4,128)(2,1)}, u32[]{:S(2)}) copy-start(bf16[4,8192]{1,0:T(4,128)(2,1)} %param.26) | copy-start | bytes 196612
  0.6 13.8 %copy-start.7 = (bf16[4,512,512]{2,1,0:T(8,128)(2,1)S(1)}, bf16[4,512,512]{2,1,0:T(8,128)(2,1)}, u32[]{:S(2)}) copy-start(bf16[4,512,512]{2,1,0:T(8,128)(2,1)} %param.17) | copy-start | bytes 6291460
  16.4 9.9 %copy-start.10 = (bf16[4,4,512]{2,1,0:T(4,128)(2,1)S(1)}, bf16[4,4,512]{2,1,0:T(4,128)(2,1)}, u32[]{:S(2)}) copy-start(bf16[4,4,512]{2,1,0:T(4,128)(2,1)} %param.19) | copy-start | bytes 49156
  19.8 3.5 %copy-start.5 = (f32[4,4,512,32,8]{2,3,4,1,0:T(8,128)}, f32[4,4,512,32,8]{2,3,4,1,0:T(8,128)S(1)}, u32[]{:S(2)}) copy-start(f32[4,4,512,32,8]{2,3,4,1,0:T(8,128)S(1)} %get-tuple-element.19) | copy-start | bytes 25165828
  19.8 7.1 %copy-start.8 = (bf16[4,512,4,128]{3,2,1,0:T(4,128)(2,1)S(1)}, bf16[4,512,4,128]{3,2,1,0:T(4,128)(2,1)}, u32[]{:S(2)}) copy-start(bf16[4,512,4,128]{3,2,1,0:T(4,128)(2,1)} %reshape.132) | copy-start | bytes 6291460
  26.3 30.4 %slice-start = ((s8[8388608]{0:T(1024)(128)(4,1)}), s8[4194304]{0:T(1024)(128)(4,1)S(1)}, s32[]{:S(2)}) async-start(s8[8388608]{0:T(1024)(128)(4,1)} %bitcast.97), calls=%async_computation | async-start | bytes 8388608
  26.9 29.8 %slice-start.1 = ((s8[8388608]{0:T(1024)(128)(4,1)}), s8[4194304]{0:T(1024)(128)(4,1)S(1)}, s32[]{:S(2)}) async-start(s8[8388608]{0:T(1024)(128)(4,1)} %bitcast.97), calls=%async_computation.1 | async-start | bytes 8388608
  26.9 29.8 %copy-start.2 = (bf16[4,32,1024]{2,1,0:T(8,128)(2,1)S(1)}, bf16[4,32,1024]{2,1,0:T(8,128)(2,1)}, u32[]{:S(2)}) copy-start(bf16[4,32,1024]{2,1,0:T(8,128)(2,1)} %param.23) | copy-start | bytes 786436
  32.0 70.6 %copy-start.9 = (s32[4,32]{1,0:T(4,128)S(1)}, s32[4,32]{1,0:T(4,128)}, u32[]{:S(2)}) copy-start(s32[4,32]{1,0:T(4,128)} %param.20) | copy-start | bytes 1540
  56.7 68.9 %copy-start.6 = (bf16[2048,1024]{1,0:T(8,128)(2,1)S(1)}, bf16[2048,1024]{1,0:T(8,128)(2,1)}, u32[]{:S(2)}) copy-start(bf16[2048,1024]{1,0:T(8,128)(2,1)} %param.27) | copy-start | bytes 12582916
  168.7 1.9 copy-start.3
  170.6 2.8 %copy-start.4 = (f32[1024,1024]{1,0:T(8,128)}, f32[1024,1024]{1,0:T(8,128)S(1)}, u32[]{:S(2)}) copy-start(f32[1024,1024]{1,0:T(8,128)S(1)} %fusion.39) | copy-start | bytes 12582916
  196.6 20.1 %copy-start.1 = (bf16[4,8192]{1,0:T(4,128)(2,1)S(1)}, bf16[4,8192]{1,0:T(4,128)(2,1)}, u32[]{:S(2)}) copy-start(bf16[4,8192]{1,0:T(4,128)(2,1)} %param.26) | copy-start | bytes 196612

commit v3 on v2

--- a/solution.py
+++ b/solution.py
@@ -328,6 +328,85 @@
     )(x)
 
 
+def settle_kernel(
+    size, terms, features, weights, all_err, pred_error, parts, passed, sums, near, far, wide, last
+):
+    me = lax.axis_index("req")
+    ys = size // 2
+    y, c = me // 2, me % 2
+    twin = y * 2 + 1 - c
+    barrier = pltpu.get_barrier_semaphore()
+    for peer in [twin] + [lax.rem(y + step, ys) * 2 + c for step in range(1, ys)]:
+        pl.semaphore_signal(barrier, inc=1, device_id={"req": peer}, device_id_type=MESH)
+    pl.semaphore_wait(barrier, ys)
+
+    def copy(src, dst, sems, step, peer):
+        return pltpu.make_async_remote_copy(
+            src_ref=src,
+            dst_ref=dst,
+            send_sem=sems.at[0, step],
+            recv_sem=sems.at[1, step],
+            device_id={"req": peer},
+            device_id_type=MESH,
+        )
+
+    def to_twin(step):
+        goal = lax.rem(y + step, ys)
+        return copy(terms.at[goal * 2 + 1 - c], parts.at[goal], near, step, twin)
+
+    def to_y(step):
+        goal = lax.rem(y + step, ys)
+        return copy(passed.at[goal], sums.at[y], far, step, goal * 2 + c)
+
+    def gather(step):
+        return copy(all_err.at[me], all_err.at[me], wide, step, lax.rem(y + step, ys) * 2 + c)
+
+    def forward(step):
+        origin = lax.rem(y + ys - step, ys) * 2 + c
+        return copy(all_err.at[origin], all_err.at[origin], last, step, twin)
+
+    steps = [*range(1, ys), 0]
+    for step in steps:
+        to_twin(step).start()
+    for step in steps:
+        goal = lax.rem(y + step, ys)
+        to_twin(step).wait()
+        total = terms[goal * 2 + c].astype(jnp.float32) + parts[goal].astype(jnp.float32)
+        if step == 0:
+            pred_error[...] = total - features[...].astype(jnp.float32)
+        else:
+            passed[goal] = total.astype(jnp.bfloat16)
+            to_y(step).start()
+    for step in range(1, ys):
+        to_y(step).wait()
+        pred_error[...] += sums[lax.rem(y + ys - step, ys)].astype(jnp.float32)
+    all_err[me] = (weights[...] * pred_error[...]).astype(jnp.bfloat16)
+    for step in range(1, ys):
+        gather(step).start()
+    forward(0).start()
+    for step in range(1, ys):
+        gather(step).wait()
+        forward(step).start()
+    for step in range(ys):
+        forward(step).wait()
+
+
+def settle(terms, features, weights, cid):
+    size, rows, width = terms.shape
+    slots = pltpu.VMEM((size // 2, rows, width), jnp.bfloat16)
+    return pl.pallas_call(
+        functools.partial(settle_kernel, size),
+        out_shape=[
+            jax.ShapeDtypeStruct((size, rows, width), jnp.bfloat16),
+            jax.ShapeDtypeStruct((rows, width), jnp.float32),
+        ],
+        in_specs=[VMEM] * 3,
+        out_specs=[VMEM] * 2,
+        scratch_shapes=[slots] * 3 + [pltpu.SemaphoreType.DMA((2, size // 2))] * 4,
+        compiler_params=params(cid),
+    )(terms, features, weights)
+
+
 def body(
     queries,
     cache_keys,
@@ -449,13 +528,8 @@
             draft_weight[piece * block_width : (piece + 1) * block_width],
             preferred_element_type=jnp.float32,
         )
-    (terms,) = exchange(
-        [terms.astype(jnp.bfloat16).reshape(reqs, row_count, block_width)], "req", 4
-    )
-    predicted = jnp.sum(terms.astype(jnp.float32), axis=0)
-    pred_error = predicted - own_block.astype(jnp.float32)
-    scaled_err = (weights * pred_error).astype(jnp.bfloat16)
-    (all_err,) = exchange([scaled_err], "req", 5, gather=True)
+    terms = terms.astype(jnp.bfloat16).reshape(reqs, row_count, block_width)
+    all_err, pred_error = settle(terms, own_block, weights, 4)
     all_err = all_err.reshape(reqs * row_count, block_width)
     gradient = jnp.concatenate(
         [

time: 218 us -> 212 us (0.972)
  Pallas kernels: 150 us -> 142 us
    pallas_call x5 -> x3, Pallas kernels: 81.6 us -> 43.1 us  [exchange(): pl.pallas_call(functools.partial(exchange_kernel, axis, size, gather, cou...]
    pallas_call x0 -> x1, Pallas kernels: none -> 30.4 us  [settle(): pl.pallas_call(functools.partial(settle_kernel, size), out_shape=[jax.Sha...]
    unnamed x29 -> x37, local copies, waits for them, and re-layouts: 6.38 us -> 6.4 us
where the time goes in v3:
time: 212 us; the launch traced here: 211 us
  Pallas kernels  142 us (67%)
  other arithmetic  31.9 us (15%)
  matrix products  18.8 us (9%)
  local copies, waits for them, and re-layouts  15.2 us (7%)
  between operations  3.64 us (2%)
    pallas_call x1, Pallas kernels, project(): pl.pallas_call(functools.partial(project_kernel, size), out_shape=jax.Sha...  45.9 us
    pallas_call x3, Pallas kernels, exchange(): pl.pallas_call(functools.partial(exchange_kernel, axis, size, gather, cou...  43.1 us
    pallas_call x1, Pallas kernels, settle(): pl.pallas_call(functools.partial(settle_kernel, size), out_shape=[jax.Sha...  30.4 us
    pallas_call x1, Pallas kernels, spread(): pl.pallas_call(functools.partial(spread_kernel, reqs, tps), out_shape=jax...  22.4 us
    convert_element_type x1, other arithmetic, body(): (draft_weight.astype(jnp.float32) - LEARN_RATE * direction).astype(jnp.bf...  19.3 us
    unnamed x37, local copies, waits for them, and re-layouts  6.4 us
    dot_general x1, matrix products, body(): jnp.einsum('rkgnc,rckd->rkgnd', cache_probs, value_view, preferred_elemen...  5.1 us

profile of v3, /device:TPU:0, one launch (start us, length us, event | category | flops | bytes accessed | tf_op | source)
XLA Modules:
  0.0 211.3 jit_solution(4472396136069962317)
XLA Ops:
  0.7 0.9 fusion.33
  2.2 1.2 broadcast_compare_fusion.1
  4.8 1.1 convolution_minimum_fusion.5
  8.6 1.5 copy.105
  10.0 2.2 %fusion.38 = (f32[4,4,8,32]{3,2,1,0:T(8,128)S(1)}, f32[4,4,8,32,4]{3,4,2,1,0:T(4,128)S(1)}) fusion(bf16[4,32,4,8,128]{4,3,2,1,0:T(8,128)(2,1)S(1)} %bitcast.114, bf16[4,4,512]{2,1,0:T(4,128)(2,1)} %param.18, pred[4,32,4]{1,2,0:T(4,128)(4,1)} %dynamic-slice_compare_fusion), kind=kOutput, calls=%fused_computation.74 | convolution fusion | flops 4239360 | bytes 1147392 | tf_op jit(solution)/shard_map/rnkgd,rjkd->rkgnj/dot_general | solution.py:444
  12.2 4.0 %reshape.131 = bf16[4,512,4,128]{3,2,1,0:T(4,128)(2,1)} reshape(bf16[4,512,512]{2,1,0:T(8,128)(2,1)} %param.16) | data formatting | bytes 4194304 | tf_op jit(solution)/shard_map/reshape | solution.py:437
  16.2 2.0 reshape.134
  18.2 3.4 %bitcast_reduce_fusion = (f32[4,4,8,32]{3,2,1,0:T(8,128)S(1)}, f32[4,4,512,32,8]{2,3,4,1,0:T(8,128)S(1)}) fusion(pred[4,512]{1,0:T(4,128)(4,1)S(1)} %broadcast_compare_fusion, bf16[4,32,4,8,128]{4,3,2,1,0:T(8,128)(2,1)S(1)} %bitcast.115, bf16[4,512,4,128,1]{3,2,1,0,4:T(4,128)(2,1)} %bitcast.112), kind=kOutput, calls=%fused_computation.4 | convolution fusion | flops 543158272 | bytes 11552768 | tf_op jit(solution)/shard_map/rnkgd,rckd->rkgnc/dot_general | solution.py:440
  21.6 3.5 %copy-done.5 = f32[4,4,512,32,8]{2,3,4,1,0:T(8,128)} copy-done((f32[4,4,512,32,8]{2,3,4,1,0:T(8,128)}, f32[4,4,512,32,8]{2,3,4,1,0:T(8,128)S(1)}, u32[]{:S(2)}) %copy-start.5) | copy-done | bytes 8388632
  25.1 2.4 %convert_reduce_fusion = f32[4,4,8,32]{3,2,1,0:T(8,128)S(1)} fusion(f32[4,4,8,32]{3,2,1,0:T(8,128)S(1)} %max.11, f32[4,4,512,32,8]{2,3,4,1,0:T(8,128)S(1)} %get-tuple-element.21, pred[4,512]{1,0:T(4,128)(4,1)S(1)} %broadcast_compare_fusion), kind=kLoop, calls=%fused_computation.11 | loop fusion | flops 14675968 | bytes 8423424 | tf_op jit(solution)/shard_map/reduce_sum | solution.py:460
  28.7 5.1 %add_convert_fusion.1 = bf16[4,4,8,32,128]{4,3,2,1,0:T(8,128)(2,1)S(1)} fusion(f32[4,4,8,32,128]{4,3,2,1,0:T(8,128)S(1)} %fusion.27, bf16[4,512,4,128,1]{3,2,1,0,4:T(4,128)(2,1)S(1)} %bitcast.111, f32[4,4,512,32,8]{2,3,4,1,0:T(8,128)} %copy-done.5, f32[4,4,8,32]{3,2,1,0:T(8,128)S(1)} %max.11, pred[4,512]{1,0:T(4,128)(4,1)S(1)} %broadcast_compare_fusion), kind=kOutput, calls=%fused_computation.23 | convolution fusion | flops 548405248 | bytes 13649920 | tf_op jit(solution)/shard_map/rkgnc,rckd->rkgnd/dot_general | solution.py:465
  34.0 23.7 %shard_map.182 = (bf16[8,512,128]{2,1,0:T(8,128)(2,1)S(1)}, f32[8,8,128]{2,1,0:T(8,128)S(1)}) custom-call(bf16[8,512,128]{2,1,0:T(8,128)(2,1)S(1)} %bitcast.99, f32[8,8,128]{2,1,0:T(8,128)S(1)} %pad_maximum_fusion.1.refs_1_), custom_call_target="tpu_custom_call" | custom-call | tf_op jit(solution)/shard_map/pallas_call | solution.py:91
  58.6 45.9 %shard_map.183.features = bf16[128,1024]{1,0:T(8,128)(2,1)S(1)} custom-call(bf16[128,512]{1,0:T(8,128)(2,1)S(1)} %bitcast.104, bf16[512,8192]{1,0:T(8,128)(2,1)S(1)} %bitcast.96, bf16[128,1024]{1,0:T(8,128)(2,1)S(1)} %bitcast.105, f32[1,1024]{1,0:T(1,128)S(1)} %bitcast.106), custom_call_target="tpu_custom_call" | custom-call | tf_op jit(solution)/shard_map/pallas_call | solution.py:190
  104.8 22.4 %shard_map.184 = bf16[4,2,128,1024]{3,2,1,0:T(8,128)(2,1)S(1)} custom-call(bf16[128,1024]{1,0:T(8,128)(2,1)S(1)} %bitcast.102), custom_call_target="tpu_custom_call" | custom-call | tf_op jit(solution)/shard_map/pallas_call | solution.py:317
  127.4 1.3 fusion.8
  128.7 1.3 add_convert_fusion
  130.0 30.4 %shard_map.185 = (bf16[4,128,1024]{2,1,0:T(8,128)(2,1)S(1)}, f32[128,1024]{1,0:T(8,128)S(1)}) custom-call(bf16[4,128,1024]{2,1,0:T(8,128)(2,1)S(1)} %bitcast.103, bf16[128,1024]{1,0:T(8,128)(2,1)S(1)} %shard_map.183.features, f32[128,1]{1,0:T(8,128)S(1)} %reshape.152.weights), custom_call_target="tpu_custom_call" | custom-call | tf_op jit(solution)/shard_map/pallas_call | solution.py:397
  161.2 1.3 fusion.40
  162.5 1.3 fusion.39
  164.5 2.8 %multiply_reduce_fusion = f32[]{:T(128)} fusion(f32[1024,1024]{1,0:T(8,128)S(1)} %fusion.40, f32[1024,1024]{1,0:T(8,128)S(1)} %fusion.39), kind=kLoop, calls=%fused_computation.10 | loop fusion | flops 6291455 | bytes 8388612 | tf_op jit(solution)/shard_map/reduce_sum | solution.py:543
  167.2 1.4 pad_maximum_fusion.2
  168.8 15.6 %shard_map.186 = f32[8,8,128]{2,1,0:T(8,128)S(1)} custom-call(f32[8,128]{1,0:T(8,128)S(1)} %broadcast_in_dim.98.refs_0_), custom_call_target="tpu_custom_call" | custom-call | tf_op jit(solution)/shard_map/pallas_call | solution.py:91
  184.5 3.7 %shard_map.187 = f32[4,8,128]{2,1,0:T(8,128)S(1)} custom-call(f32[8,128]{1,0:T(8,128)S(1)} %reduce_sum.78.refs_0_), custom_call_target="tpu_custom_call" | custom-call | tf_op jit(solution)/shard_map/pallas_call | solution.py:91
  190.1 19.3 %subtract_convert_fusion = (bf16[2048,1024]{1,0:T(8,128)(2,1)}, f32[2048,1024]{1,0:T(8,128)}, f32[2048,1024]{1,0:T(8,128)}) fusion(bf16[2048,1024]{1,0:T(8,128)(2,1)} %param.27, f32[]{:T(128)} %bitcast.32, f32[1024,1024]{1,0:T(8,128)} %copy-done.3, f32[1024,1024]{1,0:T(8,128)} %copy-done.4, f32[2048,1024]{1,0:T(8,128)} %param.28, f32[2048,1024]{1,0:T(8,128)} %param.29), kind=kLoop, calls=%fused_computation.8 | loop fusion | flops 35651584 | bytes 50331652 | tf_op jit(solution)/shard_map/convert_element_type | solution.py:556
  (76 shorter events, 10.1 us)
Async XLA Ops:
  0.6 4.2 %copy-start = (bf16[4,8192]{1,0:T(4,128)(2,1)S(1)}, bf16[4,8192]{1,0:T(4,128)(2,1)}, u32[]{:S(2)}) copy-start(bf16[4,8192]{1,0:T(4,128)(2,1)} %param.26) | copy-start | bytes 196612
  0.6 15.5 %copy-start.7 = (bf16[4,512,512]{2,1,0:T(8,128)(2,1)S(1)}, bf16[4,512,512]{2,1,0:T(8,128)(2,1)}, u32[]{:S(2)}) copy-start(bf16[4,512,512]{2,1,0:T(8,128)(2,1)} %param.17) | copy-start | bytes 6291460
  18.2 9.4 %copy-start.10 = (pred[4,32,4]{1,2,0:T(4,128)(4,1)S(1)}, pred[4,32,4]{1,2,0:T(4,128)(4,1)}, u32[]{:S(2)}) copy-start(pred[4,32,4]{1,2,0:T(4,128)(4,1)} %dynamic-slice_compare_fusion) | copy-start | bytes 1540
  21.6 3.6 %copy-start.5 = (f32[4,4,512,32,8]{2,3,4,1,0:T(8,128)}, f32[4,4,512,32,8]{2,3,4,1,0:T(8,128)S(1)}, u32[]{:S(2)}) copy-start(f32[4,4,512,32,8]{2,3,4,1,0:T(8,128)S(1)} %get-tuple-element.21) | copy-start | bytes 25165828
  21.6 6.6 %copy-start.11 = (pred[4,32,4]{1,2,0:T(4,128)(4,1)S(1)}, pred[4,32,4]{1,2,0:T(4,128)(4,1)}, u32[]{:S(2)}) copy-start(pred[4,32,4]{1,2,0:T(4,128)(4,1)} %dynamic-slice_compare_fusion) | copy-start | bytes 1540
  21.6 6.6 %copy-start.12 = (bf16[4,4,512]{2,1,0:T(4,128)(2,1)S(1)}, bf16[4,4,512]{2,1,0:T(4,128)(2,1)}, u32[]{:S(2)}) copy-start(bf16[4,4,512]{2,1,0:T(4,128)(2,1)} %param.19) | copy-start | bytes 49156
  21.6 7.1 %copy-start.8 = (bf16[4,512,4,128]{3,2,1,0:T(4,128)(2,1)S(1)}, bf16[4,512,4,128]{3,2,1,0:T(4,128)(2,1)}, u32[]{:S(2)}) copy-start(bf16[4,512,4,128]{3,2,1,0:T(4,128)(2,1)} %reshape.134) | copy-start | bytes 6291460
  28.2 30.4 %slice-start = ((s8[8388608]{0:T(1024)(128)(4,1)}), s8[4194304]{0:T(1024)(128)(4,1)S(1)}, s32[]{:S(2)}) async-start(s8[8388608]{0:T(1024)(128)(4,1)} %bitcast.95), calls=%async_computation | async-start | bytes 8388608
  28.7 29.9 %slice-start.1 = ((s8[8388608]{0:T(1024)(128)(4,1)}), s8[4194304]{0:T(1024)(128)(4,1)S(1)}, s32[]{:S(2)}) async-start(s8[8388608]{0:T(1024)(128)(4,1)} %bitcast.95), calls=%async_computation.1 | async-start | bytes 8388608
  28.7 29.9 %copy-start.2 = (bf16[4,32,1024]{2,1,0:T(8,128)(2,1)S(1)}, bf16[4,32,1024]{2,1,0:T(8,128)(2,1)}, u32[]{:S(2)}) copy-start(bf16[4,32,1024]{2,1,0:T(8,128)(2,1)} %param.23) | copy-start | bytes 786436
  33.9 70.6 %copy-start.9 = (s32[4,32]{1,0:T(4,128)S(1)}, s32[4,32]{1,0:T(4,128)}, u32[]{:S(2)}) copy-start(s32[4,32]{1,0:T(4,128)} %param.20) | copy-start | bytes 1540
  33.9 70.6 %copy-start.13 = (pred[4,32]{1,0:T(4,128)(4,1)S(1)}, pred[4,32]{1,0:T(4,128)(4,1)}, u32[]{:S(2)}) copy-start(pred[4,32]{1,0:T(4,128)(4,1)} %broadcast_compare_fusion.1) | copy-start | bytes 388
  58.5 68.9 %copy-start.6 = (bf16[2048,1024]{1,0:T(8,128)(2,1)S(1)}, bf16[2048,1024]{1,0:T(8,128)(2,1)}, u32[]{:S(2)}) copy-start(bf16[2048,1024]{1,0:T(8,128)(2,1)} %param.27) | copy-start | bytes 12582916
  127.4 33.0 %copy-start.14 = (f32[128]{0:T(128)S(1)}, f32[128]{0:T(128)}, u32[]{:S(2)}) copy-start(f32[128]{0:T(128)} %mul.129) | copy-start | bytes 1540
  162.5 1.9 copy-start.3
  164.5 2.8 %copy-start.4 = (f32[1024,1024]{1,0:T(8,128)}, f32[1024,1024]{1,0:T(8,128)S(1)}, u32[]{:S(2)}) copy-start(f32[1024,1024]{1,0:T(8,128)S(1)} %fusion.39) | copy-start | bytes 12582916
  190.1 20.1 %copy-start.1 = (bf16[4,8192]{1,0:T(4,128)(2,1)S(1)}, bf16[4,8192]{1,0:T(4,128)(2,1)}, u32[]{:S(2)}) copy-start(bf16[4,8192]{1,0:T(4,128)(2,1)} %param.26) | copy-start | bytes 196612
